TPU v7x, 32 devices: a whole 2x2x4 slice. The times are simulated.
32 devices in a mesh: pp: 2 (over core), ep: 4 (over z), tp: 4 (over y, x).
Axes of the slice: x: 2, y: 2, z: 4, core: 2. Of those that a mesh axis runs over, the one named last changes fastest.
Arguments:
- tokens: bfloat16 [2, 512, 4096], P('pp', 'ep'), may hold values from -300 to 300
- routes: int32 [2, 512, 8], P('pp', 'ep'), may hold values from 0 to 63, all different within a row; in each aligned block of 32 rows (0 to 31, 32 to 63, ..., all dimensions but the last counted through in order) at most 6 rows name the same one
- gates: float32 [2, 512, 8], P('pp', 'ep'), may hold values from 0.05 to 0.5
- norm_gain: bfloat16 [2, 4096], P('pp'), may hold values from 0.099609375 to 1.8984375
- w_gate: bfloat16 [2, 64, 768, 4096], P('pp', 'ep', 'tp'), may hold values from -0.09375 to 0.09375
- w_up: bfloat16 [2, 64, 768, 4096], P('pp', 'ep', 'tp'), may hold values from -0.09375 to 0.09375
- w_down: bfloat16 [2, 64, 768, 4096], P('pp', 'ep', 'tp'), may hold values from -0.21875 to 0.21875
Outputs:
- expert_mix: bfloat16 [2, 512, 4096], P('pp', ('ep', 'tp'))
- handoff_payload: bfloat16 [2, 512, 4096], P('pp', ('ep', 'tp'))
- handoff_scale: bfloat16 [2, 512, 32], P('pp', ('ep', 'tp'))
Inputs may be any that keep to these rules, and one draw needn't show every extreme that they name: `routes`: in each aligned block of 32 consecutive tokens of a section no expert is chosen more than 6 times; in some blocks one expert is chosen exactly 6 times.
All inputs are finite; a program needn't handle non-finite values. Where the computation divides by a largest or mean magnitude, that divisor is 1e-20 or more.
Results may differ from a plain program's by a relative error of at most 0.012.
Values may be sent and summed in bfloat16 or wider, within the bound.
A program may use at most 256 MiB of HBM per device.

v0:
```python
import jax
import jax.numpy as jnp
from jax import lax
from jax.sharding import PartitionSpec as P

TOP = 8
BLOCK = 128


def passed_along(value, axis, steps):
    count = lax.axis_size(axis)
    pairs = [(source, (source + steps) % count) for source in range(count)]
    return lax.ppermute(value, axis, pairs)


def slot_ids(block_routes, experts, capacity):
    flat = block_routes.reshape(-1)
    onehot = (flat[:, None] == jnp.arange(experts, dtype=jnp.int32)[None, :]).astype(jnp.int32)
    earlier = jnp.cumsum(onehot, axis=0) - onehot
    return flat * capacity + jnp.sum(earlier * onehot, axis=1)


def dispatch_rows(block_routes, block_rows, experts, capacity):
    count, topk = block_routes.shape
    slots = slot_ids(block_routes, experts, capacity).reshape(count, topk)
    table = jnp.sum(
        (
            slots[:, :, None] == jnp.arange(experts * capacity, dtype=jnp.int32)[None, None, :]
        ).astype(jnp.int32),
        axis=1,
    )
    return jnp.einsum(
        "ts,td->sd", table.astype(jnp.bfloat16), block_rows, preferred_element_type=jnp.float32
    ).astype(jnp.bfloat16)


def per_device(tokens, routes, gates, norm_gain, w_gate, w_up, w_down):
    parts = lax.axis_size("tp")
    rank = lax.axis_index("tp")
    peers = lax.axis_size("ep")
    local_experts = w_gate.shape[1]
    ff_part = w_gate.shape[2]
    width = tokens.shape[2]
    experts = local_experts * peers
    share = tokens.shape[1] // parts
    capacity = min(share, max(2, 3 * share * TOP // (2 * experts)))
    gate_dev = w_gate[0]
    up_dev = w_up[0]
    down_dev = w_down[0]
    source = tokens[0].astype(jnp.float32)
    inverse = lax.rsqrt(jnp.mean(source * source, axis=1, keepdims=True) + 1e-06)
    normed = (source * inverse * norm_gain[0].astype(jnp.float32)[None, :]).astype(jnp.bfloat16)
    route_all = routes[0]
    my_routes = lax.dynamic_slice_in_dim(route_all, rank * share, share, 0)
    my_gates = lax.dynamic_slice_in_dim(gates[0], rank * share, share, 0)

    def block_dispatch(block_routes, block_rows):
        return dispatch_rows(block_routes, block_rows, experts, capacity)

    outgoing = jax.vmap(block_dispatch)(
        route_all.reshape(parts, share, TOP), normed.reshape(parts, share, width)
    )
    outgoing = outgoing.reshape(parts, peers, local_experts * capacity, width)
    piece = lax.all_to_all(outgoing, "ep", split_axis=1, concat_axis=1, tiled=True)
    count = piece.shape[0]
    rows = piece.reshape(count, peers, local_experts, capacity, width)
    gate_pre = jnp.einsum("qslmd,lfd->qslmf", rows, gate_dev, preferred_element_type=jnp.float32)
    up_pre = jnp.einsum("qslmd,lfd->qslmf", rows, up_dev, preferred_element_type=jnp.float32)
    hidden = (jax.nn.silu(gate_pre) * up_pre).astype(jnp.bfloat16)
    hidden_flat = hidden.reshape(-1, ff_part)
    mine = hidden_flat.shape[0] // parts
    picked_rows = hidden_flat
    picked_rows = picked_rows.reshape(-1, local_experts, capacity, ff_part)
    term = jnp.einsum("almf,lfd->almd", picked_rows, down_dev, preferred_element_type=jnp.float32)
    summed = lax.psum_scatter(
        term.reshape(mine * lax.axis_size("tp"), width).astype(jnp.bfloat16),
        "tp",
        scatter_dimension=0,
        tiled=True,
    )
    expert_out = summed.reshape(peers, local_experts * capacity, width)
    returned = lax.all_to_all(expert_out, "ep", split_axis=0, concat_axis=0, tiled=True).reshape(
        experts * capacity, width
    )
    slots = slot_ids(my_routes, experts, capacity)
    picked = jnp.take(returned, slots, axis=0).reshape(share, TOP, width).astype(jnp.float32)
    mixed = jnp.sum(my_gates[:, :, None] * picked, axis=1)
    full = lax.dynamic_slice_in_dim(source, rank * share, share, 0) + mixed
    blocked = full.reshape(share, width // BLOCK, BLOCK)
    scale = (jnp.max(jnp.abs(blocked), axis=2) + 1e-06).astype(jnp.bfloat16)
    payload = (
        (blocked / scale.astype(jnp.float32)[:, :, None]).astype(jnp.bfloat16).reshape(share, width)
    )
    payload_in, scale_in = passed_along((payload, scale), "pp", 1)
    return (mixed.astype(jnp.bfloat16)[None], payload_in[None], scale_in[None])


def solution(mesh):
    return jax.shard_map(
        per_device,
        mesh=mesh,
        in_specs=(
            P("pp", "ep", None),
            P("pp", "ep", None),
            P("pp", "ep", None),
            P("pp", None),
            P("pp", "ep", "tp", None),
            P("pp", "ep", "tp", None),
            P("pp", "ep", "tp", None),
        ),
        out_specs=(
            P("pp", ("ep", "tp"), None),
            P("pp", ("ep", "tp"), None),
            P("pp", ("ep", "tp"), None),
        ),
        check_vma=False,
    )
```

profile of v0, /device:TPU:0, one launch (start us, length us, event | category | flops | bytes accessed | tf_op | source)
XLA Modules:
  0.0 630.2 jit_solution(8420266672048982431)
XLA Ops:
  7.2 0.0 reduce-scatter.2.cloned.1.call-start
  7.2 0.9 copy.74
  8.1 0.1 eq.72
  8.2 0.1 eq.68
  8.3 0.7 broadcast_multiply_fusion.1
  9.0 2.8 convert_element_type.106
  11.8 0.3 multiply_reduce_fusion.1
  12.1 2.4 reduce-window.16
  14.5 0.1 slice.19
  14.7 0.1 copy.79
  14.8 0.2 fusion.20
  15.0 0.1 reduce_sum.54
  15.1 0.1 copy.76
  15.2 0.5 convert_reduce_fusion
  15.8 0.1 rsqrt.12
  15.9 5.1 convolution_convert_fusion
  20.9 2.0 copy.82
  23.0 279.0 %all_to_all.10 = bf16[4,4,96,4096]{3,2,0,1:T(8,128)(2,1)S(1)} all-to-all(bf16[4,4,96,4096]{3,2,0,1:T(8,128)(2,1)S(1)} %copy.82), channel_id=1, replica_groups=mesh['pp'=2,'ep'=4,'tp'=4] {'ep'}, dimensions={1} | all-to-all | bytes 25165824 | tf_op jit(solution)/shard_map/all_to_all | solution.py:64
  302.0 28.1 %copy.83 = bf16[4,4,96,4096]{3,1,2,0:T(4,128)(2,1)} copy(bf16[4,4,96,4096]{3,2,0,1:T(8,128)(2,1)S(1)} %all_to_all.10) | data formatting | bytes 25165824 | tf_op jit(solution)/shard_map/all_to_all | solution.py:64
  330.1 16.5 %fusion.2 = f32[16,4,4,6,192]{4,2,3,1,0:T(4,128)S(1)} fusion(bf16[1,16,192,4096]{3,2,1,0:T(8,128)(2,1)} %param.12, bf16[4,4,16,6,4096]{4,1,3,2,0:T(4,128)(2,1)} %bitcast.125), kind=kOutput, calls=%fused_computation.3 | convolution fusion | flops 2415919104 | bytes 38928384 | tf_op jit(solution)/shard_map/qslmd,lfd->qslmf/dot_general | solution.py:68
  346.7 17.7 %fusion.4 = f32[16,4,4,6,192]{4,2,3,1,0:T(4,128)} fusion(bf16[1,16,192,4096]{3,2,1,0:T(8,128)(2,1)} %param.11, bf16[4,4,16,6,4096]{4,1,3,2,0:T(4,128)(2,1)} %bitcast.126), kind=kOutput, calls=%fused_computation.5 | convolution fusion | flops 2415919104 | bytes 38928384 | tf_op jit(solution)/shard_map/qslmd,lfd->qslmf/dot_general | solution.py:67
  364.4 3.3 fusion.10
  367.6 13.7 %convert_bitcast_fusion = bf16[16,16,6,4096]{3,0,2,1:T(8,128)(2,1)} fusion(bf16[1,16,192,4096]{3,2,1,0:T(8,128)(2,1)} %param.13, bf16[16,16,6,192]{3,1,2,0:T(8,128)(2,1)S(1)} %bitcast.127), kind=kOutput, calls=%fused_computation.7 | convolution fusion | flops 2422210560 | bytes 38338560 | tf_op jit(solution)/shard_map/almf,lfd->almd/dot_general | solution.py:74
  381.3 13.8 %copy.89 = bf16[16,16,6,4096]{3,2,1,0:T(8,128)(2,1)} copy(bf16[16,16,6,4096]{3,0,2,1:T(8,128)(2,1)} %convert_bitcast_fusion) | data formatting | bytes 25165824 | tf_op jit(solution)/shard_map/convert_element_type | solution.py:76
  395.1 18.8 %convert_element_type.99 = bf16[1536,4096]{1,0:T(8,128)(2,1)} reshape(bf16[16,16,6,4096]{3,2,1,0:T(8,128)(2,1)} %copy.89) | data formatting | bytes 25165824 | tf_op jit(solution)/shard_map/convert_element_type | solution.py:76
  414.0 120.8 %reduce-scatter.2.cloned.1.call-done = bf16[384,4096]{1,0:T(8,128)(2,1)} async-done(((bf16[1536,4096]{1,0:T(8,128)(2,1)}), bf16[384,4096]{1,0:T(8,128)(2,1)}) %reduce-scatter.2.cloned.1.call-update) | async-done | bytes 3145744 | tf_op jit(solution)/shard_map/reduce_scatter | solution.py:75
  534.8 4.6 all-to-all-start.1
  539.3 0.1 eq.64
  539.4 0.1 reshape.165
  539.5 0.6 reduce-window.14
  540.2 0.2 slice_reduce_fusion
  540.4 0.1 mul.109
  540.5 0.1 fusion.25
  540.6 0.1 reduce_sum.52
  540.7 0.1 dynamic-slice_bitcast_fusion
  540.8 0.1 copy.73
  540.9 69.1 %all-to-all-done.1 = bf16[4,96,4096]{2,1,0:T(8,128)(2,1)S(1)} async-done(((bf16[4,96,4096]{2,1,0:T(8,128)(2,1)}), bf16[4,96,4096]{2,1,0:T(8,128)(2,1)S(1)}, u32[]{:S(2)}, u32[]{:S(2)}) %all-to-all-start.1) | async-done | bytes 3145760 | tf_op jit(solution)/shard_map/all_to_all | solution.py:82
  610.0 3.2 gather_fusion
  613.2 3.5 multiply_reduce_fusion
  616.7 1.2 abs_bitcast_fusion
  617.9 0.1 copy.95
  618.0 0.2 reduce_max.9
  618.2 0.2 div.24
  618.4 2.1 fusion.17
  620.5 0.5 collective-permute-start.1
  621.0 1.0 collective-permute-done.1
  622.1 0.7 copy.110
  622.8 0.6 copy.111
  (24 shorter events, 0.2 us)
Async XLA Ops:
  7.2 533.5 %copy-start = (f32[1,128,8]{1,2,0:T(8,128)S(1)}, f32[1,128,8]{1,2,0:T(8,128)}, u32[]{:S(2)}) copy-start(f32[1,128,8]{1,2,0:T(8,128)} %param.9) | copy-start | bytes 12292
  7.2 4.6 copy-start.1
  7.2 527.6 %reduce-scatter.2.cloned.1.call-start = ((), (), s32[]{:S(2)}) async-start(), calls=%async_computation.3 | async-start | bytes 15728640 | tf_op jit(solution)/shard_map/reduce_scatter | solution.py:75
  9.0 6.7 %copy-start.2 = (bf16[1,4096]{1,0:T(2,128)(2,1)S(1)}, bf16[1,4096]{1,0:T(2,128)(2,1)}, u32[]{:S(2)}) copy-start(bf16[1,4096]{1,0:T(2,128)(2,1)} %param.10) | copy-start | bytes 24580
  534.8 75.3 %all-to-all-start.1 = ((bf16[4,96,4096]{2,1,0:T(8,128)(2,1)}), bf16[4,96,4096]{2,1,0:T(8,128)(2,1)S(1)}, u32[]{:S(2)}, u32[]{:S(2)}) async-start(bf16[4,96,4096]{2,1,0:T(8,128)(2,1)} %bitcast.128), calls=%async_computation.2 | async-start | bytes 6291456 | tf_op jit(solution)/shard_map/all_to_all | solution.py:82
  620.5 1.6 collective-permute-start
  620.5 1.5 collective-permute-start.1
Sparse Core Ops, SparseCore 0:
  414.1 120.6 reduce-scatter.1
where the time goes:
time: 631 us; the launch traced here: 630 us
  blocking collectives  279 us (44%)
  waiting for transfers between devices  191 us (30%)
  local copies, waits for them, and re-layouts  69.9 us (11%)
  matrix products  53 us (8%)
  other arithmetic  18 us (3%)
  between operations  14.2 us (2%)
    all_to_all x1, blocking collectives, per_device(): lax.all_to_all(outgoing, 'ep', split_axis=1, concat_axis=1, tiled=True)  279 us
    reduce_scatter x1, waiting for transfers between devices, per_device(): lax.psum_scatter(term.reshape(mine * lax.axis_size('tp'), width).astype(j...  121 us
    all_to_all x1, waiting for transfers between devices, per_device(): lax.all_to_all(expert_out, 'ep', split_axis=0, concat_axis=0, tiled=True)  69.1 us
    convert_element_type x2, local copies, waits for them, and re-layouts, per_device(): term.reshape(mine * lax.axis_size('tp'), width).astype(jnp.bfloat16)  32.6 us
    all_to_all x1, local copies, waits for them, and re-layouts, per_device(): lax.all_to_all(outgoing, 'ep', split_axis=1, concat_axis=1, tiled=True)  28.1 us
    dot_general x1, matrix products, per_device(): jnp.einsum('qslmd,lfd->qslmf', rows, gate_dev, preferred_element_type=jnp...  17.7 us
    dot_general x1, matrix products, per_device(): jnp.einsum('qslmd,lfd->qslmf', rows, up_dev, preferred_element_type=jnp.f...  16.5 us
    dot_general x1, matrix products, per_device(): jnp.einsum('almf,lfd->almd', picked_rows, down_dev, preferred_element_typ...  13.7 us
  transfers between devices with their start and end apart: 4, of which 3 were waited for; matrix products, arithmetic and copies ran while one was open for 0% of the time, Pallas kernels for 0%

commit v1 on v0

v1 whole, which is shorter than its diff:
```python
import jax
import jax.numpy as jnp
from jax import lax
from jax.sharding import PartitionSpec as P

TOP = 8
BLOCK = 128
EXTRA = 128


def passed_along(value, axis, steps):
    count = lax.axis_size(axis)
    pairs = [(source, (source + steps) % count) for source in range(count)]
    return lax.ppermute(value, axis, pairs)


def per_device(tokens, routes, gates, norm_gain, w_gate, w_up, w_down):
    parts = lax.axis_size("tp")
    rank = lax.axis_index("tp")
    peers = lax.axis_size("ep")
    local = w_gate.shape[1]
    ff_part = w_gate.shape[2]
    width = tokens.shape[2]
    experts = local * peers
    share = tokens.shape[1] // parts
    total = share * parts * peers
    blocks = parts * peers
    capacity = min(share, max(2, 3 * share * TOP // (2 * experts)))
    first_expert = lax.axis_index("ep") * local

    source = lax.dynamic_slice_in_dim(tokens[0], rank * share, share, 0).astype(jnp.float32)
    inverse = lax.rsqrt(jnp.mean(source * source, axis=1, keepdims=True) + 1e-06)
    normed = (source * inverse * norm_gain[0].astype(jnp.float32)[None, :]).astype(jnp.bfloat16)
    my_routes = lax.dynamic_slice_in_dim(routes[0], rank * share, share, 0)
    my_gates = lax.dynamic_slice_in_dim(gates[0], rank * share, share, 0)
    small = jnp.concatenate([my_routes.astype(jnp.float32), my_gates], axis=1)
    small_all = lax.all_gather(small, ("ep", "tp"), axis=0, tiled=True)
    rows_all = lax.all_gather(normed, ("ep", "tp"), axis=0, tiled=True)

    route_all = small_all[:, :TOP].astype(jnp.int32)
    gate_all = small_all[:, TOP:]
    mine = first_expert + jnp.arange(local, dtype=jnp.int32)
    match = route_all[:, :, None] == mine[None, None, :]
    chosen = jnp.any(match, axis=1)
    weight = jnp.sum(jnp.where(match, gate_all[:, :, None], 0.0), axis=1)
    counted = chosen.astype(jnp.int32).reshape(blocks, share, local)
    earlier = (jnp.cumsum(counted, axis=1) - counted).reshape(total, local)
    base = (jnp.arange(total, dtype=jnp.int32) // share * capacity)[:, None]
    slot = jnp.where(chosen, base + earlier, -1)
    table = (
        slot.T[:, None, :] == jnp.arange(blocks * capacity, dtype=jnp.int32)[None, :, None]
    )
    table16 = table.astype(jnp.bfloat16)
    slot_gate = jnp.sum(jnp.where(table, weight.T[:, None, :], 0.0), axis=2)
    rows = jnp.einsum("lst,td->lsd", table16, rows_all, preferred_element_type=jnp.float32)
    rows = rows.astype(jnp.bfloat16)
    gate_pre = jnp.einsum("lsd,lfd->lsf", rows, w_gate[0], preferred_element_type=jnp.float32)
    up_pre = jnp.einsum("lsd,lfd->lsf", rows, w_up[0], preferred_element_type=jnp.float32)
    hidden = (jax.nn.silu(gate_pre) * up_pre * slot_gate[:, :, None]).astype(jnp.bfloat16)
    spread = jnp.einsum("lst,lsf->tlf", table16, hidden, preferred_element_type=jnp.float32)
    spread = spread.astype(jnp.bfloat16).reshape(total, local * ff_part)
    part = jnp.dot(
        spread, w_down[0].reshape(local * ff_part, width), preferred_element_type=jnp.float32
    ).astype(jnp.bfloat16)
    mixed = lax.psum_scatter(part, ("ep", "tp"), scatter_dimension=0, tiled=True)
    mixed = mixed.astype(jnp.float32)
    full = source + mixed
    blocked = full.reshape(share, width // BLOCK, BLOCK)
    scale = (jnp.max(jnp.abs(blocked), axis=2) + 1e-06).astype(jnp.bfloat16)
    payload = (
        (blocked / scale.astype(jnp.float32)[:, :, None]).astype(jnp.bfloat16).reshape(share, width)
    )
    payload_in, scale_in = passed_along((payload, scale), "pp", 1)
    return (mixed.astype(jnp.bfloat16)[None], payload_in[None], scale_in[None])


def solution(mesh):
    return jax.shard_map(
        per_device,
        mesh=mesh,
        in_specs=(
            P("pp", "ep", None),
            P("pp", "ep", None),
            P("pp", "ep", None),
            P("pp", None),
            P("pp", "ep", "tp", None),
            P("pp", "ep", "tp", None),
            P("pp", "ep", "tp", None),
        ),
        out_specs=(
            P("pp", ("ep", "tp"), None),
            P("pp", ("ep", "tp"), None),
            P("pp", ("ep", "tp"), None),
        ),
        check_vma=False,
    )
```

time: 631 us -> 262 us (0.42)
  blocking collectives: 279 us -> 43.7 us
  local copies, waits for them, and re-layouts: 69.9 us -> 2.37 us
  waiting for transfers between devices: 191 us -> 126 us
  matrix products: 53 us -> 65.1 us
  other arithmetic: 18 us -> 9.49 us
    all_to_all x1 -> x0, blocking collectives: 279 us -> none  [per_device(): lax.all_to_all(outgoing, 'ep', split_axis=1, concat_axis=1, tiled=True)]
    all_to_all x1 -> x0, waiting for transfers between devices: 69.1 us -> none  [per_device(): lax.all_to_all(expert_out, 'ep', split_axis=0, concat_axis=0, tiled=True)]
    all_gather x0 -> x1, blocking collectives: none -> 43.7 us  [per_device(): small_all = lax.all_gather(small, ('ep', 'tp'), axis=0, tiled=True)]
    convert_element_type x2, local copies, waits for them, and re-layouts: 32.6 us -> 0.27 us  [per_device(): counted = chosen.astype(jnp.int32).reshape(blocks, share, local)]
    all_gather x0 -> x1, waiting for transfers between devices: none -> 31.5 us  [per_device(): rows_all = lax.all_gather(normed, ('ep', 'tp'), axis=0, tiled=True)]
    all_to_all x1 -> x0, local copies, waits for them, and re-layouts: 28.1 us -> none  [per_device(): lax.all_to_all(outgoing, 'ep', split_axis=1, concat_axis=1, tiled=True)]
    reduce_scatter x1, waiting for transfers between devices: 121 us -> 93.9 us  [per_device(): lax.psum_scatter(part, ('ep', 'tp'), scatter_dimension=0, tiled=True)]
    dot_general x4, matrix products: 53 us -> 65.1 us  [the longest x1 20.4 us: per_device(): jnp.dot(spread, w_down[0].reshape(local * ff_part, width), preferred_elem...]
  transfers between devices with their start and end apart: 4 -> 4, of which waited for: 3 -> 3; matrix products, arithmetic and copies ran while one was open for 0% -> 2% of each run, Pallas kernels for 0% -> 0%
where the time goes in v1:
time: 262 us
  waiting for transfers between devices  126 us (48%)
  matrix products  65.1 us (25%)
  blocking collectives  43.7 us (17%)
  between operations  14.2 us (5%)
  other arithmetic  9.49 us (4%)
    reduce_scatter x1, waiting for transfers between devices, per_device(): lax.psum_scatter(part, ('ep', 'tp'), scatter_dimension=0, tiled=True)  93.9 us
    all_gather x1, blocking collectives, per_device(): small_all = lax.all_gather(small, ('ep', 'tp'), axis=0, tiled=True)  43.7 us
    all_gather x1, waiting for transfers between devices, per_device(): rows_all = lax.all_gather(normed, ('ep', 'tp'), axis=0, tiled=True)  31.5 us
    dot_general x1, matrix products, per_device(): jnp.dot(spread, w_down[0].reshape(local * ff_part, width), preferred_elem...  20.4 us
    dot_general x1, matrix products, per_device(): jnp.einsum('lst,lsf->tlf', table16, hidden, preferred_element_type=jnp.fl...  17.4 us
    dot_general x1, matrix products, per_device(): jnp.einsum('lsd,lfd->lsf', rows, w_gate[0], preferred_element_type=jnp.fl...  15.6 us
    dot_general x1, matrix products, per_device(): jnp.einsum('lst,td->lsd', table16, rows_all, preferred_element_type=jnp.f...  11.8 us
  transfers between devices with their start and end apart: 4, of which 3 were waited for; matrix products, arithmetic and copies ran while one was open for 2% of the time, Pallas kernels for 0%

profile of v1, /device:TPU:0, one launch (start us, length us, event | category | flops | bytes accessed | tf_op | source)
XLA Modules:
  0.0 262.0 jit_solution(6337785107525182915)
XLA Ops:
  7.2 0.0 copy-start
  7.2 0.0 all-gather.3.cloned.1.call-start
  7.2 1.1 fusion.11
  8.4 0.7 mul.72
  9.1 1.8 fusion.13
  10.9 0.0 all-gather.3.cloned.1.call-update
  10.9 0.0 reduce-scatter.2.cloned.1.call-start
  11.0 0.8 convert_bitcast_fusion
  11.7 0.0 copy-done
  11.7 0.1 dynamic-slice_bitcast_fusion
  11.8 43.7 %all-gather = f32[16,32,16]{1,2,0:T(8,128)S(1)} all-gather(f32[1,32,16]{1,2,0:T(8,128)S(1)} %maximum_bitcast_fusion), channel_id=1, replica_groups=mesh['pp'=2,'ep'=4,'tp'=4] {'ep','tp'}, dimensions={0}, use_global_device_ids=true | all-gather | bytes 34816 | tf_op jit(solution)/shard_map/all_gather | solution.py:37
  55.6 0.1 reshape.66
  55.7 0.1 compare_reduce_fusion
  55.9 0.1 reshape.62
  55.9 0.2 copy.24
  56.1 1.9 fusion.24
  58.0 0.2 copy.25
  58.2 0.1 reduce_window_sum.14
  58.3 0.1 fusion.15
  58.4 0.4 select_reduce_fusion
  58.8 31.5 %all-gather.3.cloned.1.call-done = bf16[512,4096]{1,0:T(8,128)(2,1)} async-done(((bf16[32,4096]{1,0:T(8,128)(2,1)}), bf16[512,4096]{1,0:T(8,128)(2,1)}) %all-gather.3.cloned.1.call-update) | async-done | bytes 4194320 | tf_op jit(solution)/shard_map/all_gather | solution.py:38
  90.4 11.8 %convolution_convert_fusion = bf16[16,96,4096]{2,1,0:T(8,128)(2,1)} fusion(bf16[512,4096]{1,0:T(8,128)(2,1)} %all-gather.3.cloned.1.call-done, s32[16,512]{1,0:T(8,128)S(1)} %select_bitcast_fusion), kind=kOutput, calls=%fused_computation.4 | convolution fusion | flops 6449528832 | bytes 16809984 | tf_op jit(solution)/shard_map/lst,td->lsd/dot_general | solution.py:55
  102.1 15.6 %fusion.2 = f32[16,96,192]{2,1,0:T(8,128)S(1)} fusion(bf16[16,96,4096]{2,1,0:T(8,128)(2,1)} %convolution_convert_fusion, bf16[1,16,192,4096]{3,2,1,0:T(8,128)(2,1)} %param.11), kind=kOutput, calls=%fused_computation.2 | convolution fusion | flops 2415919104 | bytes 38928384 | tf_op jit(solution)/shard_map/lsd,lfd->lsf/dot_general | solution.py:57
  117.7 17.4 %fusion.6 = bf16[16,192,512]{2,1,0:T(8,128)(2,1)} fusion(s32[16,512]{1,0:T(8,128)S(1)} %select_bitcast_fusion, f32[16,96,192]{2,1,0:T(8,128)S(1)} %fusion.2, bf16[16,96,4096]{2,1,0:T(8,128)(2,1)} %convolution_convert_fusion, bf16[1,16,192,4096]{3,2,1,0:T(8,128)(2,1)} %param.12, f32[16,96]{1,0:T(8,128)S(1)} %select_reduce_fusion), kind=kOutput, calls=%fused_computation.10 | convolution fusion | flops 2722332672 | bytes 42113024 | tf_op jit(solution)/shard_map/lst,lsf->tlf/dot_general | solution.py:60
  135.1 20.4 %convolution_convert_fusion.1 = bf16[512,4096]{1,0:T(8,128)(2,1)} fusion(bf16[512,3072]{0,1:T(8,128)(2,1)} %bitcast.63, bf16[3072,4096]{1,0:T(8,128)(2,1)} %bitcast.62), kind=kOutput, calls=%fused_computation.5 | convolution fusion | flops 12886999040 | bytes 32505856 | tf_op jit(solution)/shard_map/dot_general | solution.py:62
  155.5 0.0 copy-start.2
  155.5 0.0 copy-start.1
  155.5 0.0 reduce-scatter.2.cloned.1.call-update
  155.5 93.9 %reduce-scatter.2.cloned.1.call-done = bf16[32,4096]{1,0:T(8,128)(2,1)} async-done(((bf16[512,4096]{1,0:T(8,128)(2,1)}), bf16[32,4096]{1,0:T(8,128)(2,1)}) %reduce-scatter.2.cloned.1.call-update) | async-done | bytes 262160 | tf_op jit(solution)/shard_map/reduce_scatter | solution.py:65
  249.4 0.0 copy-done.2
  249.4 1.0 abs_bitcast_fusion
  250.4 0.1 copy.28
  250.5 0.2 reduce_max.9
  250.7 0.2 div.34
  250.9 1.3 fusion.14
  252.2 0.1 collective-permute-start
  252.3 0.5 collective-permute-start.1
  252.8 1.0 collective-permute-done.1
  253.8 0.0 collective-permute-done
  253.9 0.7 copy.33
  254.6 0.6 copy.34
  255.2 0.0 copy-done.1
  (9 shorter events, 0.1 us)
Async XLA Ops:
  7.2 4.6 %copy-start = (f32[1,128,8]{1,2,0:T(8,128)S(1)}, f32[1,128,8]{1,2,0:T(8,128)}, u32[]{:S(2)}) copy-start(f32[1,128,8]{1,2,0:T(8,128)} %param.9) | copy-start | bytes 12292
  7.2 83.2 %all-gather.3.cloned.1.call-start = ((), (), s32[]{:S(2)}) async-start(), calls=%async_computation.1 | async-start | bytes 4456448 | tf_op jit(solution)/shard_map/all_gather | solution.py:38
  10.9 238.5 %reduce-scatter.2.cloned.1.call-start = ((), (), s32[]{:S(2)}) async-start(), calls=%async_computation.2 | async-start | bytes 4456448 | tf_op jit(solution)/shard_map/reduce_scatter | solution.py:65
  155.5 93.9 %copy-start.2 = (bf16[1,128,4096]{2,1,0:T(8,128)(2,1)S(1)}, bf16[1,128,4096]{2,1,0:T(8,128)(2,1)}, u32[]{:S(2)}) copy-start(bf16[1,128,4096]{2,1,0:T(8,128)(2,1)} %param.7) | copy-start | bytes 3145732
  155.5 99.7 %copy-start.1 = (f32[1,128,8]{1,2,0:T(8,128)S(1)}, f32[1,128,8]{1,2,0:T(8,128)}, u32[]{:S(2)}) copy-start(f32[1,128,8]{1,2,0:T(8,128)} %param.9) | copy-start | bytes 12292
  252.2 1.6 collective-permute-start
  252.3 1.5 collective-permute-start.1
Sparse Core Ops, SparseCore 0:
  11.4 78.9 all-gather.2
  155.6 93.7 reduce-scatter.1

commit v2 on v1

v2 whole, which is shorter than its diff:
```python
import functools

import jax
import jax.numpy as jnp
from jax import lax
from jax.experimental import pallas as pl
from jax.experimental.pallas import tpu as pltpu
from jax.sharding import PartitionSpec as P

TOP = 8
BLOCK = 128
EXTRA = 128
CHUNK = 512
PAIR = 2
LAG = 2
MESH = pl.DeviceIdType.MESH


def passed_along(value, axis, steps):
    count = lax.axis_size(axis)
    pairs = [(source, (source + steps) % count) for source in range(count)]
    return lax.ppermute(value, axis, pairs)


def hidden_kernel(width, slots, rows_ref, slot_row_ref, weight_row_ref, slot_col_ref, gate_ref, up_ref, out_ref):
    step = pl.program_id(0)
    group, _, total = slot_row_ref.shape
    ff_part = gate_ref.shape[1]
    tables = []
    scales = []
    for i in range(group):
        hit = lax.broadcasted_iota(jnp.int32, (slots, total), 0) == slot_row_ref[i]
        tables.append(hit.astype(jnp.float32).astype(jnp.bfloat16))
        scales.append(jnp.sum(jnp.where(hit, weight_row_ref[i], 0.0), axis=1, keepdims=True))
    rows = jnp.dot(
        jnp.concatenate(tables, axis=0), rows_ref[:, :width], preferred_element_type=jnp.float32
    ).astype(jnp.bfloat16)
    contract = (((1,), (1,)), ((), ()))
    slot_col = slot_col_ref[...]
    lane = lax.broadcasted_iota(jnp.int32, slot_col.shape, 1)
    for i in range(group):
        mine = rows[i * slots:(i + 1) * slots]
        gate_pre = lax.dot_general(mine, gate_ref[i], contract, preferred_element_type=jnp.float32)
        up_pre = lax.dot_general(mine, up_ref[i], contract, preferred_element_type=jnp.float32)
        hidden = gate_pre / (1.0 + jnp.exp(-gate_pre)) * up_pre * scales[i]
        column = jnp.sum(
            jnp.where(lane == step * group + i, slot_col, 0), axis=1, keepdims=True
        )
        back = lax.broadcasted_iota(jnp.int32, (total, slots), 1) == column
        spread = jnp.dot(
            back.astype(jnp.float32).astype(jnp.bfloat16),
            hidden.astype(jnp.bfloat16),
            preferred_element_type=jnp.float32,
        )
        out_ref[:, i * ff_part:(i + 1) * ff_part] = spread.astype(jnp.bfloat16)


def hidden_spread(rows_all, slot, weight, slot_out, w_gate, w_up, slots):
    total, local = slot.shape
    ff_part, width = w_gate.shape[1:]
    return pl.pallas_call(
        functools.partial(hidden_kernel, width, slots),
        out_shape=jax.ShapeDtypeStruct((total, local * ff_part), jnp.bfloat16),
        grid=(local // PAIR,),
        in_specs=[
            pl.BlockSpec(rows_all.shape, lambda i: (0, 0)),
            pl.BlockSpec((PAIR, 1, total), lambda i: (i, 0, 0)),
            pl.BlockSpec((PAIR, 1, total), lambda i: (i, 0, 0)),
            pl.BlockSpec((total, local), lambda i: (0, 0)),
            pl.BlockSpec((PAIR, ff_part, width), lambda i: (i, 0, 0)),
            pl.BlockSpec((PAIR, ff_part, width), lambda i: (i, 0, 0)),
        ],
        out_specs=pl.BlockSpec((total, PAIR * ff_part), lambda i: (0, i)),
        compiler_params=pltpu.CompilerParams(vmem_limit_bytes=50 * 2**20),
        name="hidden_spread",
    )(rows_all, slot.T[:, None, :], weight.T[:, None, :], slot_out, w_gate, w_up)


def down_kernel(groups, peers, spread_ref, w_ref, out_ref, w_buf, send1, recv1, send2, recv2, w_sem, s1, r1, s2, r2):
    chunks = send1.shape[0]
    group_rows = send2.shape[1]
    block_rows = recv2.shape[2]
    me_tp = lax.axis_index("tp")
    me_ep = lax.axis_index("ep")

    def load(c):
        slot = lax.rem(c, 3)
        columns = pl.ds(pl.multiple_of(c * CHUNK, CHUNK), CHUNK)
        return pltpu.make_async_copy(w_ref.at[:, columns], w_buf.at[slot], w_sem.at[slot])

    def first(c, k):
        peer = lax.rem(me_tp + k, groups)
        return pltpu.make_async_remote_copy(
            src_ref=send1.at[c, pl.ds(pl.multiple_of(peer * group_rows, group_rows), group_rows)],
            dst_ref=recv1.at[c, k - 1],
            send_sem=s1.at[c, k - 1],
            recv_sem=r1.at[c, k - 1],
            device_id={"tp": peer},
            device_id_type=MESH,
        )

    def second(c, k):
        peer = lax.rem(me_ep + k, peers)
        return pltpu.make_async_remote_copy(
            src_ref=send2.at[c, pl.ds(pl.multiple_of(peer * block_rows, block_rows), block_rows)],
            dst_ref=recv2.at[c, k - 1],
            send_sem=s2.at[c, k - 1],
            recv_sem=r2.at[c, k - 1],
            device_id={"ep": peer},
            device_id_type=MESH,
        )

    load(0).start()
    load(1).start()
    barrier = pltpu.get_barrier_semaphore()
    for k in range(1, groups):
        pl.semaphore_signal(
            barrier, inc=1, device_id={"tp": lax.rem(me_tp + k, groups)}, device_id_type=MESH
        )
    for k in range(1, peers):
        pl.semaphore_signal(
            barrier, inc=1, device_id={"ep": lax.rem(me_ep + k, peers)}, device_id_type=MESH
        )
    pl.semaphore_wait(barrier, groups + peers - 2)

    def step(c, carry):
        @pl.when(c < chunks)
        def _():
            load(c).wait()

            @pl.when(c + 2 < chunks)
            def _():
                load(c + 2).start()

            send1[c] = jnp.dot(
                spread_ref[...], w_buf[lax.rem(c, 3)], preferred_element_type=jnp.float32
            ).astype(jnp.bfloat16)
            for k in range(1, groups):
                first(c, k).start()

        @pl.when((c >= LAG) & (c < chunks + LAG))
        def _():
            d = c - LAG
            own = pl.ds(pl.multiple_of(me_tp * group_rows, group_rows), group_rows)
            value = send1[d, own].astype(jnp.float32)
            for k in range(1, groups):
                first(d, k).wait_recv()
                value = value + recv1[d, k - 1].astype(jnp.float32)
            send2[d] = value.astype(jnp.bfloat16)
            for k in range(1, peers):
                second(d, k).start()

        @pl.when(c >= 2 * LAG)
        def _():
            d = c - 2 * LAG
            own = pl.ds(pl.multiple_of(me_ep * block_rows, block_rows), block_rows)
            value = send2[d, own].astype(jnp.float32)
            for k in range(1, peers):
                second(d, k).wait_recv()
                value = value + recv2[d, k - 1].astype(jnp.float32)
            out_ref[:, pl.ds(pl.multiple_of(d * CHUNK, CHUNK), CHUNK)] = value

        return carry

    lax.fori_loop(0, chunks + 2 * LAG, step, 0)

    def drain(c, carry):
        for k in range(1, groups):
            first(c, k).wait_send()
        for k in range(1, peers):
            second(c, k).wait_send()
        return carry

    lax.fori_loop(0, chunks, drain, 0)


def down_scatter(spread, w_down, groups, peers):
    total, depth = spread.shape
    width = w_down.shape[1]
    chunks = width // CHUNK
    group_rows = total // groups
    block_rows = group_rows // peers
    return pl.pallas_call(
        functools.partial(down_kernel, groups, peers),
        out_shape=jax.ShapeDtypeStruct((block_rows, width), jnp.float32),
        in_specs=[pl.BlockSpec(memory_space=pltpu.VMEM), pl.BlockSpec(memory_space=pl.ANY)],
        out_specs=pl.BlockSpec(memory_space=pltpu.VMEM),
        scratch_shapes=[
            pltpu.VMEM((3, depth, CHUNK), jnp.bfloat16),
            pltpu.VMEM((chunks, total, CHUNK), jnp.bfloat16),
            pltpu.VMEM((chunks, groups - 1, group_rows, CHUNK), jnp.bfloat16),
            pltpu.VMEM((chunks, group_rows, CHUNK), jnp.bfloat16),
            pltpu.VMEM((chunks, peers - 1, block_rows, CHUNK), jnp.bfloat16),
            pltpu.SemaphoreType.DMA((3,)),
            pltpu.SemaphoreType.DMA((chunks, groups - 1)),
            pltpu.SemaphoreType.DMA((chunks, groups - 1)),
            pltpu.SemaphoreType.DMA((chunks, peers - 1)),
            pltpu.SemaphoreType.DMA((chunks, peers - 1)),
        ],
        compiler_params=pltpu.CompilerParams(
            collective_id=0, has_side_effects=True, vmem_limit_bytes=50 * 2**20
        ),
        name="down_scatter",
    )(spread, w_down)


def per_device(tokens, routes, gates, norm_gain, w_gate, w_up, w_down):
    parts = lax.axis_size("tp")
    rank = lax.axis_index("tp")
    peers = lax.axis_size("ep")
    local = w_gate.shape[1]
    ff_part = w_gate.shape[2]
    width = tokens.shape[2]
    experts = local * peers
    share = tokens.shape[1] // parts
    total = share * parts * peers
    blocks = parts * peers
    capacity = min(share, max(2, 3 * share * TOP // (2 * experts)))
    first_expert = lax.axis_index("ep") * local

    source = lax.dynamic_slice_in_dim(tokens[0], rank * share, share, 0).astype(jnp.float32)
    inverse = lax.rsqrt(jnp.mean(source * source, axis=1, keepdims=True) + 1e-06)
    normed = (source * inverse * norm_gain[0].astype(jnp.float32)[None, :]).astype(jnp.bfloat16)
    my_routes = lax.dynamic_slice_in_dim(routes[0], rank * share, share, 0)
    my_gates = lax.dynamic_slice_in_dim(gates[0], rank * share, share, 0)
    gate_high = lax.reduce_precision(my_gates, 8, 7)
    small = jnp.concatenate(
        [
            my_routes.astype(jnp.bfloat16),
            gate_high.astype(jnp.bfloat16),
            (my_gates - gate_high).astype(jnp.bfloat16),
            jnp.zeros((share, EXTRA - 3 * TOP), jnp.bfloat16),
        ],
        axis=1,
    )
    packed = jnp.concatenate([normed, small], axis=1)
    rows_all = lax.all_gather(packed, ("ep", "tp"), axis=0, tiled=True)
    small_all = rows_all[:, width:width + 3 * TOP].astype(jnp.float32)
    route_all = small_all[:, :TOP].astype(jnp.int32)
    gate_all = small_all[:, TOP:2 * TOP] + small_all[:, 2 * TOP:]
    mine = first_expert + jnp.arange(local, dtype=jnp.int32)
    match = route_all[:, :, None] == mine[None, None, :]
    chosen = jnp.any(match, axis=1)
    weight = jnp.sum(jnp.where(match, gate_all[:, :, None], 0.0), axis=1)
    counted = chosen.astype(jnp.int32).reshape(blocks, share, local)
    earlier = (jnp.cumsum(counted, axis=1) - counted).reshape(total, local)
    base = (jnp.arange(total, dtype=jnp.int32) // share * capacity)[:, None]
    slot = jnp.where(chosen, base + earlier, -1)
    if total * width <= 2**22 and local % PAIR == 0 and width % CHUNK == 0:
        slot_out = slot.reshape(peers, parts, share, local).swapaxes(0, 1).reshape(total, local)
        spread = hidden_spread(
            rows_all, slot, weight, slot_out, w_gate[0], w_up[0], blocks * capacity
        )
        mixed = down_scatter(spread, w_down[0].reshape(local * ff_part, width), parts, peers)
    else:
        table = (
            slot.T[:, None, :] == jnp.arange(blocks * capacity, dtype=jnp.int32)[None, :, None]
        )
        table16 = table.astype(jnp.bfloat16)
        slot_gate = jnp.sum(jnp.where(table, weight.T[:, None, :], 0.0), axis=2)
        rows = jnp.einsum("lst,td->lsd", table16, rows_all[:, :width], preferred_element_type=jnp.float32)
        rows = rows.astype(jnp.bfloat16)
        gate_pre = jnp.einsum("lsd,lfd->lsf", rows, w_gate[0], preferred_element_type=jnp.float32)
        up_pre = jnp.einsum("lsd,lfd->lsf", rows, w_up[0], preferred_element_type=jnp.float32)
        hidden = (jax.nn.silu(gate_pre) * up_pre * slot_gate[:, :, None]).astype(jnp.bfloat16)
        spread = jnp.einsum("lst,lsf->tlf", table16, hidden, preferred_element_type=jnp.float32)
        spread = spread.astype(jnp.bfloat16).reshape(total, local * ff_part)
        part = jnp.dot(
            spread, w_down[0].reshape(local * ff_part, width), preferred_element_type=jnp.float32
        ).astype(jnp.bfloat16)
        mixed = lax.psum_scatter(part, ("ep", "tp"), scatter_dimension=0, tiled=True)
    mixed = mixed.astype(jnp.float32)
    full = source + mixed
    blocked = full.reshape(share, width // BLOCK, BLOCK)
    scale = (jnp.max(jnp.abs(blocked), axis=2) + 1e-06).astype(jnp.bfloat16)
    payload = (
        (blocked / scale.astype(jnp.float32)[:, :, None]).astype(jnp.bfloat16).reshape(share, width)
    )
    payload_in, scale_in = passed_along((payload, scale), "pp", 1)
    return (mixed.astype(jnp.bfloat16)[None], payload_in[None], scale_in[None])


def solution(mesh):
    return jax.shard_map(
        per_device,
        mesh=mesh,
        in_specs=(
            P("pp", "ep", None),
            P("pp", "ep", None),
            P("pp", "ep", None),
            P("pp", None),
            P("pp", "ep", "tp", None),
            P("pp", "ep", "tp", None),
            P("pp", "ep", "tp", None),
        ),
        out_specs=(
            P("pp", ("ep", "tp"), None),
            P("pp", ("ep", "tp"), None),
            P("pp", ("ep", "tp"), None),
        ),
        check_vma=False,
    )
```

time: 262 us -> 196 us (0.75)
  Pallas kernels: 0 us -> 88.2 us
  matrix products: 65.1 us -> 0 us
  waiting for transfers between devices: 126 us -> 80.9 us
  blocking collectives: 43.7 us -> 0 us
    reduce_scatter x1 -> x0, waiting for transfers between devices: 93.9 us -> none  [per_device(): lax.psum_scatter(part, ('ep', 'tp'), scatter_dimension=0, tiled=True)]
    pallas_call x0 -> x2, Pallas kernels: none -> 88.2 us  [the longest x1 56.2 us: down_scatter(): pl.pallas_call(functools.partial(down_kernel, groups, peers), out_shape=j...]
    dot_general x4 -> x0, matrix products: 65.1 us -> none  [the longest x1 20.4 us: per_device(): jnp.dot(spread, w_down[0].reshape(local * ff_part, width), preferred_elem...]
    all_gather x1, waiting for transfers between devices: 31.5 us -> 79.8 us  [per_device(): rows_all = lax.all_gather(packed, ('ep', 'tp'), axis=0, tiled=True)]
    all_gather x1 -> x0, blocking collectives: 43.7 us -> none  [per_device(): small_all = lax.all_gather(small, ('ep', 'tp'), axis=0, tiled=True)]
  transfers between devices with their start and end apart: 4 -> 3, of which waited for: 3 -> 2; matrix products, arithmetic and copies ran while one was open for 2% -> 0% of each run, Pallas kernels for 0% -> 0%
where the time goes in v2:
time: 196 us
  Pallas kernels  88.2 us (45%)
  waiting for transfers between devices  80.9 us (41%)
  between operations  14.3 us (7%)
  other arithmetic  7.67 us (4%)
  local copies, waits for them, and re-layouts  4.46 us (2%)
    all_gather x1, waiting for transfers between devices, per_device(): rows_all = lax.all_gather(packed, ('ep', 'tp'), axis=0, tiled=True)  79.8 us
    pallas_call x1, Pallas kernels, down_scatter(): pl.pallas_call(functools.partial(down_kernel, groups, peers), out_shape=j...  56.2 us
    pallas_call x1, Pallas kernels, hidden_spread(): pl.pallas_call(functools.partial(hidden_kernel, width, slots), out_shape=...  32 us
  transfers between devices with their start and end apart: 3, of which 2 were waited for; matrix products, arithmetic and copies ran while one was open for 0% of the time, Pallas kernels for 0%

profile of v2, /device:TPU:0, one launch (start us, length us, event | category | flops | bytes accessed | tf_op | source)
XLA Modules:
  0.0 196.0 jit_solution(5597382018946613113)
XLA Ops:
  7.2 0.0 copy-start
  7.2 0.0 all-gather.2.cloned.1.call-start
  7.2 1.1 fusion
  8.4 0.0 copy-done
  8.4 0.1 constant_dynamic-slice_fusion.1
  8.4 0.8 constant_dynamic-slice_fusion
  9.2 0.1 copy.27
  9.3 0.1 copy.35
  9.4 0.7 mul.60
  10.1 1.1 fusion.2
  11.2 0.8 concatenate.3
  12.0 0.0 all-gather.2.cloned.1.call-update
  12.1 79.8 %all-gather.2.cloned.1.call-done.rows_ref = bf16[512,4224]{1,0:T(8,128)(2,1)} async-done(((bf16[32,4224]{1,0:T(8,128)(2,1)}), bf16[512,4224]{1,0:T(8,128)(2,1)}) %all-gather.2.cloned.1.call-update) | async-done | bytes 4325392 | tf_op jit(solution)/shard_map/all_gather | solution.py:237
  91.9 0.9 slice_convert_fusion.1
  92.8 0.2 slice_add_fusion
  93.0 0.1 copy.28
  93.1 0.1 compare_reduce_fusion
  93.3 0.1 reduce_or.12
  93.4 0.1 copy.31
  93.5 0.1 fusion.4
  93.6 0.2 copy.34
  93.8 0.1 reshape.72
  93.9 0.2 copy.29
  94.1 1.9 fusion.14
  96.0 0.2 copy.30
  96.2 0.1 reduce_window_sum.16
  96.3 0.1 fusion.6
  96.5 0.0 copy-start.1
  96.5 32.0 %hidden_spread.1.spread_ref = bf16[512,3072]{1,0:T(8,128)(2,1)S(1)} custom-call(bf16[512,4224]{1,0:T(8,128)(2,1)} %all-gather.2.cloned.1.call-done.rows_ref, s32[16,1,512]{2,1,0:T(1,128)S(1)} %broadcast_in_dim.45.slot_row_ref, f32[16,1,512]{2,1,0:T(1,128)S(1)} %broadcast_in_dim.48.weight_row_ref, s32[512,16]{1,0:T(8,128)S(1)} %bitcast.41, ...), custom_call_target="tpu_custom_call" | custom-call | tf_op jit(solution)/shard_map/hidden_spread/pallas_call | solution.py:61
  128.5 0.0 copy-start.2
  128.5 56.2 %down_scatter.1 = f32[32,4096]{1,0:T(8,128)S(1)} custom-call(bf16[512,3072]{1,0:T(8,128)(2,1)S(1)} %hidden_spread.1.spread_ref, bf16[3072,4096]{1,0:T(8,128)(2,1)} %bitcast.44), custom_call_target="tpu_custom_call" | custom-call | tf_op jit(solution)/shard_map/down_scatter/pallas_call | solution.py:183
  184.7 0.0 copy-done.2
  184.7 0.1 abs_bitcast_fusion
  184.8 0.1 copy.36
  184.9 0.2 reduce_max.9
  185.1 0.2 div.35
  185.3 1.0 fusion.3
  186.3 0.0 collective-permute-start
  186.3 0.5 collective-permute-start.1
  186.8 1.0 collective-permute-done.1
  187.9 0.0 collective-permute-done
  187.9 0.7 copy.46
  188.6 0.6 copy.47
  189.2 0.0 copy-done.1
  (12 shorter events, 0.1 us)
Async XLA Ops:
  7.2 1.2 copy-start
  7.2 84.7 %all-gather.2.cloned.1.call-start = ((), (), s32[]{:S(2)}) async-start(), calls=%async_computation | async-start | bytes 4595712 | tf_op jit(solution)/shard_map/all_gather | solution.py:237
  96.5 92.7 %copy-start.1 = (s32[1,128,8]{1,2,0:T(8,128)S(1)}, s32[1,128,8]{1,2,0:T(8,128)}, u32[]{:S(2)}) copy-start(s32[1,128,8]{1,2,0:T(8,128)} %param.8) | copy-start | bytes 12292
  128.5 56.2 %copy-start.2 = (bf16[1,128,4096]{2,1,0:T(8,128)(2,1)S(1)}, bf16[1,128,4096]{2,1,0:T(8,128)(2,1)}, u32[]{:S(2)}) copy-start(bf16[1,128,4096]{2,1,0:T(8,128)(2,1)} %param.7) | copy-start | bytes 3145732
  186.3 1.6 collective-permute-start
  186.3 1.5 collective-permute-start.1
Sparse Core Ops, SparseCore 0:
  12.1 79.7 all-gather.1
